TPU v7x, 32 devices: a whole 2x2x4 slice. The times are simulated.
32 devices in a mesh: grp: 2 (over x), blk: 8 (over z, y), sum: 2 (over core).
Axes of the slice: x: 2, y: 2, z: 4, core: 2. Of those that a mesh axis runs over, the one named last changes fastest.
Arguments:
- points: bfloat16 [32768, 512], P(('grp', 'blk')), parts along dimension 0, may hold values from -6 to 6
- centers: bfloat16 [2048, 512], P(('blk', 'sum')), may hold values from -6 to 6
- coefficients: bfloat16 [2048, 256], P(('blk', 'sum')), may hold values from -60 to 60
- targets: float32 [32768, 256], P(('grp', 'blk'), 'sum'), parts along dimension 0, may hold values from -6 to 6
Outputs:
- residual: float32 [32768, 256], P(('grp', 'blk'), 'sum'), parts along dimension 0
There are 2 independent parts, one for each index of `grp`. A program takes and returns all parts, laid end to end along the dimension named above; an argument that names none is the same for every part. Nothing has to cross between parts.
All inputs are finite; a program needn't handle non-finite values.
Results may differ from a plain program's by a relative error of at most 0.0029.
Values may be sent and summed in bfloat16 or wider, within the bound.
A program may use at most 64 MiB of HBM per device.

v0:
```python
import math
import jax
import jax.numpy as jnp
from jax import lax
from jax.sharding import PartitionSpec as P


def kernel_sum(points, point_sq, sharpness, center_block, coef_block):
    products = lax.dot_general(
        points, center_block, (((1,), (1,)), ((), ())), preferred_element_type=jnp.float32
    )
    center_sq = jnp.sum(jnp.square(center_block.astype(jnp.float32)), axis=1)
    kernel = jnp.exp(-sharpness * (point_sq[:, None] + center_sq[None, :] - 2.0 * products)).astype(
        jnp.bfloat16
    )
    return jnp.dot(kernel, coef_block, preferred_element_type=jnp.float32)


def per_device(points, centers, coefficients, targets):
    features = points.shape[1]
    sharpness = 0.15 / math.sqrt(features)
    point_sq = jnp.sum(jnp.square(points.astype(jnp.float32)), axis=1)
    start_sum = jnp.zeros((points.shape[0], coefficients.shape[1]), jnp.float32)
    center_piece = lax.all_gather(centers, "blk", axis=0, tiled=True)
    coef_piece = lax.all_gather(coefficients, "blk", axis=0, tiled=True)
    piece_rows = center_piece.shape[0]
    block_rows = math.gcd(piece_rows, 256)
    block_count = piece_rows // block_rows
    center_blocks = center_piece.reshape(block_count, block_rows, features)
    coef_blocks = coef_piece.reshape(block_count, block_rows, coef_piece.shape[1])

    def step(inner_sum, blocks):
        return (inner_sum + kernel_sum(points, point_sq, sharpness, blocks[0], blocks[1]), None)

    result, _ = lax.scan(step, start_sum, (center_blocks, coef_blocks))
    predicted = lax.psum_scatter(result, "sum", scatter_dimension=1, tiled=True)
    return targets - predicted


def solution(mesh):
    return jax.shard_map(
        per_device,
        mesh=mesh,
        in_specs=(
            P(("grp", "blk"), None),
            P(("blk", "sum"), None),
            P(("blk", "sum"), None),
            P(("grp", "blk"), "sum"),
        ),
        out_specs=P(("grp", "blk"), "sum"),
        check_vma=False,
    )
```

profile of v0, /device:TPU:0, one launch (start us, length us, event | category | flops | bytes accessed | tf_op | source)
XLA Modules:
  0.0 91.5 jit_solution(9340841907587885446)
XLA Ops:
  6.5 0.0 copy-start
  6.5 0.0 all-gather.2.cloned.1.call-start
  6.5 0.7 all-gather.2.cloned.1.call-update
  7.3 0.0 reduce-scatter.2.cloned.1.call-start
  7.3 33.7 %all_gather.7 = bf16[1024,256]{1,0:T(8,128)(2,1)S(1)} all-gather(bf16[128,256]{1,0:T(8,128)(2,1)} %param.8), channel_id=1, replica_groups=mesh['grp'=2,'blk'=8,'sum'=2] {'blk'}, dimensions={0}, use_global_device_ids=true | all-gather | bytes 589824 | tf_op jit(solution)/shard_map/all_gather | solution.py:25
  41.1 2.1 %multiply_reduce_fusion.1 = f32[2048]{0:T(1024)S(1)} fusion(bf16[2048,512]{1,0:T(8,128)(2,1)} %param.6), kind=kLoop, calls=%fused_computation.19 | loop fusion | flops 3143680 | bytes 2105344 | tf_op jit(solution)/shard_map/reduce_sum | solution.py:22
  43.1 9.7 %all-gather.2.cloned.1.call-done = bf16[1024,512]{1,0:T(8,128)(2,1)} async-done(((bf16[128,512]{1,0:T(8,128)(2,1)}), bf16[1024,512]{1,0:T(8,128)(2,1)}) %all-gather.2.cloned.1.call-update) | async-done | bytes 1048592 | tf_op jit(solution)/shard_map/all_gather | solution.py:24
  52.8 0.0 copy-done
  52.8 20.6 %while.11 = (s32[]{:T(128)}, f32[2048,256]{1,0:T(8,128)}, f32[2048]{0:T(1024)S(1)}, bf16[4,256,512]{2,1,0:T(8,128)(2,1)}, bf16[2048,512]{1,0:T(8,128)(2,1)S(1)},...) while((s32[]{:T(128)}, f32[2048,256]{1,0:T(8,128)}, f32[2048]{0:T(1024)S(1)}, ...), condition=%wide.region_3.4_spmd.clone, body=%wide.region_1.3_spmd.clone.sunk | while | flops 809369344 | bytes 6958179 | solution.py:35
  52.8 1.1 %multiply_reduce_fusion.3 = f32[256]{0:T(256)S(1)} fusion(bf16[4,256,512]{2,1,0:T(8,128)(2,1)} %get-tuple-element.127, s32[]{:T(128)} %get-tuple-element.116), kind=kLoop, calls=%fused_computation.11.clone.1 | loop fusion | flops 392960 | bytes 263172 | tf_op jit(solution)/shard_map/while/body/eval_jaxpr/reduce_sum | solution.py:12
  53.9 3.5 %convolution_add_fusion.2 = f32[2048,256]{1,0:T(8,128)} fusion(f32[2048,256]{1,0:T(8,128)} %get-tuple-element.117, bf16[2048,512]{1,0:T(8,128)(2,1)S(1)} %get-tuple-element.128, f32[256]{0:T(256)S(1)} %multiply_reduce_fusion.3, f32[2048]{0:T(1024)S(1)} %get-tuple-element.126, pred[]{:T(512)S(6)} %compare.3, ...), kind=kOutput, calls=%fused_computation.5.clone.1 | convolution fusion | flops 808976384 | bytes 6694913 | tf_op jit(solution)/shard_map/while/body/eval_jaxpr/dot_general | solution.py:16
  57.4 1.1 %multiply_reduce_fusion.3 = f32[256]{0:T(256)S(1)} fusion(bf16[4,256,512]{2,1,0:T(8,128)(2,1)} %get-tuple-element.127, s32[]{:T(128)} %get-tuple-element.116), kind=kLoop, calls=%fused_computation.11.clone.1 | loop fusion | flops 392960 | bytes 263172 | tf_op jit(solution)/shard_map/while/body/eval_jaxpr/reduce_sum | solution.py:12
  58.5 4.2 %convolution_add_fusion.2 = f32[2048,256]{1,0:T(8,128)} fusion(f32[2048,256]{1,0:T(8,128)} %get-tuple-element.117, bf16[2048,512]{1,0:T(8,128)(2,1)S(1)} %get-tuple-element.128, f32[256]{0:T(256)S(1)} %multiply_reduce_fusion.3, f32[2048]{0:T(1024)S(1)} %get-tuple-element.126, pred[]{:T(512)S(6)} %compare.3, ...), kind=kOutput, calls=%fused_computation.5.clone.1 | convolution fusion | flops 808976384 | bytes 6694913 | tf_op jit(solution)/shard_map/while/body/eval_jaxpr/dot_general | solution.py:16
  62.8 1.1 %multiply_reduce_fusion.3 = f32[256]{0:T(256)S(1)} fusion(bf16[4,256,512]{2,1,0:T(8,128)(2,1)} %get-tuple-element.127, s32[]{:T(128)} %get-tuple-element.116), kind=kLoop, calls=%fused_computation.11.clone.1 | loop fusion | flops 392960 | bytes 263172 | tf_op jit(solution)/shard_map/while/body/eval_jaxpr/reduce_sum | solution.py:12
  63.9 4.2 %convolution_add_fusion.2 = f32[2048,256]{1,0:T(8,128)} fusion(f32[2048,256]{1,0:T(8,128)} %get-tuple-element.117, bf16[2048,512]{1,0:T(8,128)(2,1)S(1)} %get-tuple-element.128, f32[256]{0:T(256)S(1)} %multiply_reduce_fusion.3, f32[2048]{0:T(1024)S(1)} %get-tuple-element.126, pred[]{:T(512)S(6)} %compare.3, ...), kind=kOutput, calls=%fused_computation.5.clone.1 | convolution fusion | flops 808976384 | bytes 6694913 | tf_op jit(solution)/shard_map/while/body/eval_jaxpr/dot_general | solution.py:16
  68.1 1.1 %multiply_reduce_fusion.3 = f32[256]{0:T(256)S(1)} fusion(bf16[4,256,512]{2,1,0:T(8,128)(2,1)} %get-tuple-element.127, s32[]{:T(128)} %get-tuple-element.116), kind=kLoop, calls=%fused_computation.11.clone.1 | loop fusion | flops 392960 | bytes 263172 | tf_op jit(solution)/shard_map/while/body/eval_jaxpr/reduce_sum | solution.py:12
  69.2 4.2 %convolution_add_fusion.2 = f32[2048,256]{1,0:T(8,128)} fusion(f32[2048,256]{1,0:T(8,128)} %get-tuple-element.117, bf16[2048,512]{1,0:T(8,128)(2,1)S(1)} %get-tuple-element.128, f32[256]{0:T(256)S(1)} %multiply_reduce_fusion.3, f32[2048]{0:T(1024)S(1)} %get-tuple-element.126, pred[]{:T(512)S(6)} %compare.3, ...), kind=kOutput, calls=%fused_computation.5.clone.1 | convolution fusion | flops 808976384 | bytes 6694913 | tf_op jit(solution)/shard_map/while/body/eval_jaxpr/dot_general | solution.py:16
  73.4 0.0 copy-start.1
  73.4 0.0 reduce-scatter.2.cloned.1.call-update
  73.5 8.9 %reduce-scatter.2.cloned.1.call-done = f32[2048,128]{1,0:T(8,128)} async-done(((f32[2048,256]{1,0:T(8,128)}), f32[2048,128]{1,0:T(8,128)}) %reduce-scatter.2.cloned.1.call-update) | async-done | bytes 1048592 | tf_op jit(solution)/shard_map/reduce_scatter | solution.py:36
  82.4 0.0 copy-done.1
  82.4 2.3 %sub.6 = f32[2048,128]{1,0:T(8,128)} subtract(f32[2048,128]{1,0:T(8,128)S(1)} %copy-done.1, f32[2048,128]{1,0:T(8,128)} %reduce-scatter.2.cloned.1.call-done) | non-fusion elementwise | flops 262144 | bytes 3145728 | tf_op jit(solution)/shard_map/sub | solution.py:37
  (1 shorter events, 0.0 us)
Async XLA Ops:
  6.5 46.3 %copy-start = (bf16[2048,512]{1,0:T(8,128)(2,1)S(1)}, bf16[2048,512]{1,0:T(8,128)(2,1)}, u32[]{:S(2)}) copy-start(bf16[2048,512]{1,0:T(8,128)(2,1)} %param.6) | copy-start | bytes 6291460
  6.5 46.3 %all-gather.2.cloned.1.call-start = ((), (), s32[]{:S(2)}) async-start(), calls=%async_computation.1 | async-start | bytes 1179648 | tf_op jit(solution)/shard_map/all_gather | solution.py:24
  7.3 75.1 %reduce-scatter.2.cloned.1.call-start = ((), (), s32[]{:S(2)}) async-start(), calls=%async_computation.2 | async-start | bytes 3145728 | tf_op jit(solution)/shard_map/reduce_scatter | solution.py:36
  73.4 8.9 %copy-start.1 = (f32[2048,128]{1,0:T(8,128)S(1)}, f32[2048,128]{1,0:T(8,128)}, u32[]{:S(2)}) copy-start(f32[2048,128]{1,0:T(8,128)} %param.9) | copy-start | bytes 3145732
Sparse Core Ops, SparseCore 0:
  9.5 43.3 all-gather.1
  73.6 8.7 reduce-scatter.1
where the time goes:
time: 91.9 us; the launch traced here: 91.5 us
  blocking collectives  33.7 us (37%)
  waiting for transfers between devices  19.3 us (21%)
  matrix products  16.2 us (18%)
  between operations  13.4 us (15%)
  other arithmetic  8.69 us (9%)
    all_gather x1, blocking collectives, per_device(): coef_piece = lax.all_gather(coefficients, 'blk', axis=0, tiled=True)  33.7 us
    dot_general x4, matrix products, kernel_sum(): return jnp.dot(kernel, coef_block, preferred_element_type=jnp.float32)  16.2 us
    all_gather x1, waiting for transfers between devices, per_device(): center_piece = lax.all_gather(centers, 'blk', axis=0, tiled=True)  9.71 us
    reduce_scatter x1, waiting for transfers between devices, per_device(): predicted = lax.psum_scatter(result, 'sum', scatter_dimension=1, tiled=True)  8.9 us
    reduce_sum x4, other arithmetic, kernel_sum(): center_sq = jnp.sum(jnp.square(center_block.astype(jnp.float32)), axis=1)  4.32 us
    sub x1, other arithmetic, per_device(): return targets - predicted  2.3 us
    reduce_sum x1, other arithmetic, per_device(): point_sq = jnp.sum(jnp.square(points.astype(jnp.float32)), axis=1)  2.08 us
  transfers between devices with their start and end apart: 2, of which 2 were waited for; matrix products, arithmetic and copies ran while one was open for 2% of the time, Pallas kernels for 0%

commit v1 on v0

--- a/solution.py
+++ b/solution.py
@@ -3,6 +3,16 @@
 import jax.numpy as jnp
 from jax import lax
 from jax.sharding import PartitionSpec as P
+
+
+def pass_along(value, axis, dim):
+    size = lax.axis_size(axis)
+    held, tiles = (value, [value])
+    for _ in range(size - 1):
+        held = lax.ppermute(held, axis, [(i, (i + 1) % size) for i in range(size)])
+        tiles.insert(0, held)
+    line = jnp.concatenate(tiles, axis=dim)
+    return jnp.roll(line, (lax.axis_index(axis) + 1) * value.shape[dim], axis=dim)
 
 
 def kernel_sum(points, point_sq, sharpness, center_block, coef_block):
@@ -22,7 +32,7 @@
     point_sq = jnp.sum(jnp.square(points.astype(jnp.float32)), axis=1)
     start_sum = jnp.zeros((points.shape[0], coefficients.shape[1]), jnp.float32)
     center_piece = lax.all_gather(centers, "blk", axis=0, tiled=True)
-    coef_piece = lax.all_gather(coefficients, "blk", axis=0, tiled=True)
+    coef_piece = pass_along(coefficients, "blk", 0)
     piece_rows = center_piece.shape[0]
     block_rows = math.gcd(piece_rows, 256)
     block_count = piece_rows // block_rows

time: 91.9 us -> 124 us (1.35)
  waiting for transfers between devices: 19.3 us -> 81.8 us
  blocking collectives: 33.7 us -> 0 us
  starting transfers between devices: 0.04 us -> 3.03 us
    ppermute x0 -> x7, waiting for transfers between devices: none -> 45.7 us  [pass_along(): held = lax.ppermute(held, axis, [(i, (i + 1) % size) for i in range(size)])]
    all_gather x1 -> x0, blocking collectives: 33.7 us -> none  [per_device(): coef_piece = lax.all_gather(coefficients, 'blk', axis=0, tiled=True)]
    all_gather x1, waiting for transfers between devices: 9.71 us -> 27.6 us  [per_device(): center_piece = lax.all_gather(centers, 'blk', axis=0, tiled=True)]
    ppermute x0 -> x7, starting transfers between devices: none -> 2.98 us  [pass_along(): held = lax.ppermute(held, axis, [(i, (i + 1) % size) for i in range(size)])]
  transfers between devices with their start and end apart: 2 -> 9, of which waited for: 2 -> 9; matrix products, arithmetic and copies ran while one was open for 2% -> 2% of each run, Pallas kernels for 0% -> 0%
where the time goes in v1:
time: 124 us
  waiting for transfers between devices  81.8 us (66%)
  matrix products  16.2 us (13%)
  between operations  13.6 us (11%)
  other arithmetic  8.69 us (7%)
  starting transfers between devices  3.03 us (2%)
    ppermute x7, waiting for transfers between devices, pass_along(): held = lax.ppermute(held, axis, [(i, (i + 1) % size) for i in range(size)])  45.7 us
    all_gather x1, waiting for transfers between devices, per_device(): center_piece = lax.all_gather(centers, 'blk', axis=0, tiled=True)  27.6 us
    dot_general x4, matrix products, kernel_sum(): return jnp.dot(kernel, coef_block, preferred_element_type=jnp.float32)  16.2 us
    reduce_scatter x1, waiting for transfers between devices, per_device(): predicted = lax.psum_scatter(result, 'sum', scatter_dimension=1, tiled=True)  8.51 us
    reduce_sum x4, other arithmetic, kernel_sum(): center_sq = jnp.sum(jnp.square(center_block.astype(jnp.float32)), axis=1)  4.32 us
    ppermute x7, starting transfers between devices, pass_along(): held = lax.ppermute(held, axis, [(i, (i + 1) % size) for i in range(size)])  2.98 us
  transfers between devices with their start and end apart: 9, of which 9 were waited for; matrix products, arithmetic and copies ran while one was open for 2% of the time, Pallas kernels for 0%

profile of v1, /device:TPU:0, one launch (start us, length us, event | category | flops | bytes accessed | tf_op | source)
XLA Modules:
  0.0 123.5 jit_solution(17929172667654986922)
XLA Ops:
  6.5 0.0 copy-start.2
  6.5 0.0 all-gather.2.cloned.1.call-start
  6.5 3.0 %collective-permute-start = (bf16[128,256]{1,0:T(8,128)(2,1)}, bf16[128,256]{1,0:T(8,128)(2,1)S(1)}, u32[]{:S(2)}, u32[]{:S(2)}) collective-permute-start(bf16[128,256]{1,0:T(8,128)(2,1)} %param.8), channel_id=1, source_target_pairs={{0,2},{2,4},{4,6},{6,8},{8,10},{10,12},{12,14},{14,0},{1,3},{3,5},... | collective-permute-start | bytes 196616 | tf_op jit(solution)/shard_map/ppermute | solution.py:12
  9.5 5.6 %collective-permute-done = bf16[128,256]{1,0:T(8,128)(2,1)S(1)} collective-permute-done((bf16[128,256]{1,0:T(8,128)(2,1)}, bf16[128,256]{1,0:T(8,128)(2,1)S(1)}, u32[]{:S(2)}, u32[]{:S(2)}) %collective-permute-start) | collective-permute-done | bytes 65568 | tf_op jit(solution)/shard_map/ppermute | solution.py:12
  15.1 0.0 collective-permute-start.1
  15.1 7.0 %collective-permute-done.1 = bf16[128,256]{1,0:T(8,128)(2,1)S(1)} collective-permute-done((bf16[128,256]{1,0:T(8,128)(2,1)S(1)}, bf16[128,256]{1,0:T(8,128)(2,1)S(1)}, u32[]{:S(2)}, u32[]{:S(2)}) %collective-permute-start.1) | collective-permute-done | bytes 65568 | tf_op jit(solution)/shard_map/ppermute | solution.py:12
  22.0 0.0 collective-permute-start.2
  22.0 7.0 %collective-permute-done.2 = bf16[128,256]{1,0:T(8,128)(2,1)S(1)} collective-permute-done((bf16[128,256]{1,0:T(8,128)(2,1)S(1)}, bf16[128,256]{1,0:T(8,128)(2,1)S(1)}, u32[]{:S(2)}, u32[]{:S(2)}) %collective-permute-start.2) | collective-permute-done | bytes 65568 | tf_op jit(solution)/shard_map/ppermute | solution.py:12
  29.0 0.0 collective-permute-start.3
  29.0 7.0 %collective-permute-done.3 = bf16[128,256]{1,0:T(8,128)(2,1)S(1)} collective-permute-done((bf16[128,256]{1,0:T(8,128)(2,1)S(1)}, bf16[128,256]{1,0:T(8,128)(2,1)S(1)}, u32[]{:S(2)}, u32[]{:S(2)}) %collective-permute-start.3) | collective-permute-done | bytes 65568 | tf_op jit(solution)/shard_map/ppermute | solution.py:12
  36.0 0.0 collective-permute-start.4
  36.0 7.4 %collective-permute-done.4 = bf16[128,256]{1,0:T(8,128)(2,1)S(1)} collective-permute-done((bf16[128,256]{1,0:T(8,128)(2,1)S(1)}, bf16[128,256]{1,0:T(8,128)(2,1)S(1)}, u32[]{:S(2)}, u32[]{:S(2)}) %collective-permute-start.4) | collective-permute-done | bytes 65568 | tf_op jit(solution)/shard_map/ppermute | solution.py:12
  43.4 0.0 collective-permute-start.5
  43.4 0.0 all-gather.2.cloned.1.call-update
  43.4 0.0 reduce-scatter.2.cloned.1.call-start
  43.4 6.9 %collective-permute-done.5 = bf16[128,256]{1,0:T(8,128)(2,1)S(1)} collective-permute-done((bf16[128,256]{1,0:T(8,128)(2,1)S(1)}, bf16[128,256]{1,0:T(8,128)(2,1)S(1)}, u32[]{:S(2)}, u32[]{:S(2)}) %collective-permute-start.5) | collective-permute-done | bytes 65568 | tf_op jit(solution)/shard_map/ppermute | solution.py:12
  50.3 0.0 collective-permute-start.6
  50.3 2.1 %multiply_reduce_fusion.1 = f32[2048]{0:T(1024)S(1)} fusion(bf16[2048,512]{1,0:T(8,128)(2,1)} %param.6), kind=kLoop, calls=%fused_computation.19 | loop fusion | flops 3143680 | bytes 2105344 | tf_op jit(solution)/shard_map/reduce_sum | solution.py:32
  52.4 0.0 copy-start
  52.4 5.0 %collective-permute-done.6 = bf16[128,256]{1,0:T(8,128)(2,1)S(1)} collective-permute-done((bf16[128,256]{1,0:T(8,128)(2,1)S(1)}, bf16[128,256]{1,0:T(8,128)(2,1)S(1)}, u32[]{:S(2)}, u32[]{:S(2)}) %collective-permute-start.6) | collective-permute-done | bytes 65568 | tf_op jit(solution)/shard_map/ppermute | solution.py:12
  57.5 0.0 copy-done.2
  57.7 27.6 %all-gather.2.cloned.1.call-done = bf16[1024,512]{1,0:T(8,128)(2,1)} async-done(((bf16[128,512]{1,0:T(8,128)(2,1)}), bf16[1024,512]{1,0:T(8,128)(2,1)}) %all-gather.2.cloned.1.call-update) | async-done | bytes 1048592 | tf_op jit(solution)/shard_map/all_gather | solution.py:34
  85.3 0.0 copy-done
  85.3 20.6 %while.11 = (s32[]{:T(128)}, f32[2048,256]{1,0:T(8,128)}, f32[2048]{0:T(1024)S(1)}, bf16[4,256,512]{2,1,0:T(8,128)(2,1)}, bf16[2048,512]{1,0:T(8,128)(2,1)S(1)},...) while((s32[]{:T(128)}, f32[2048,256]{1,0:T(8,128)}, f32[2048]{0:T(1024)S(1)}, ...), condition=%wide.region_3.4_spmd.clone, body=%wide.region_1.3_spmd.clone.sunk | while | flops 809369344 | bytes 6958179 | solution.py:45
  85.3 1.1 multiply_reduce_fusion.3
  86.3 3.5 %convolution_add_fusion.2 = f32[2048,256]{1,0:T(8,128)} fusion(f32[2048,256]{1,0:T(8,128)} %get-tuple-element.117, bf16[2048,512]{1,0:T(8,128)(2,1)S(1)} %get-tuple-element.128, f32[256]{0:T(256)S(1)} %multiply_reduce_fusion.3, f32[2048]{0:T(1024)S(1)} %get-tuple-element.126, pred[]{:T(512)S(6)} %compare.4, ...), kind=kOutput, calls=%fused_computation.5.clone.1 | convolution fusion | flops 808976384 | bytes 6694913 | tf_op jit(solution)/shard_map/while/body/eval_jaxpr/dot_general | solution.py:26
  89.9 1.1 multiply_reduce_fusion.3
  90.9 4.2 %convolution_add_fusion.2 = f32[2048,256]{1,0:T(8,128)} fusion(f32[2048,256]{1,0:T(8,128)} %get-tuple-element.117, bf16[2048,512]{1,0:T(8,128)(2,1)S(1)} %get-tuple-element.128, f32[256]{0:T(256)S(1)} %multiply_reduce_fusion.3, f32[2048]{0:T(1024)S(1)} %get-tuple-element.126, pred[]{:T(512)S(6)} %compare.4, ...), kind=kOutput, calls=%fused_computation.5.clone.1 | convolution fusion | flops 808976384 | bytes 6694913 | tf_op jit(solution)/shard_map/while/body/eval_jaxpr/dot_general | solution.py:26
  95.2 1.1 multiply_reduce_fusion.3
  96.3 4.2 %convolution_add_fusion.2 = f32[2048,256]{1,0:T(8,128)} fusion(f32[2048,256]{1,0:T(8,128)} %get-tuple-element.117, bf16[2048,512]{1,0:T(8,128)(2,1)S(1)} %get-tuple-element.128, f32[256]{0:T(256)S(1)} %multiply_reduce_fusion.3, f32[2048]{0:T(1024)S(1)} %get-tuple-element.126, pred[]{:T(512)S(6)} %compare.4, ...), kind=kOutput, calls=%fused_computation.5.clone.1 | convolution fusion | flops 808976384 | bytes 6694913 | tf_op jit(solution)/shard_map/while/body/eval_jaxpr/dot_general | solution.py:26
  100.5 1.1 multiply_reduce_fusion.3
  101.6 4.2 %convolution_add_fusion.2 = f32[2048,256]{1,0:T(8,128)} fusion(f32[2048,256]{1,0:T(8,128)} %get-tuple-element.117, bf16[2048,512]{1,0:T(8,128)(2,1)S(1)} %get-tuple-element.128, f32[256]{0:T(256)S(1)} %multiply_reduce_fusion.3, f32[2048]{0:T(1024)S(1)} %get-tuple-element.126, pred[]{:T(512)S(6)} %compare.4, ...), kind=kOutput, calls=%fused_computation.5.clone.1 | convolution fusion | flops 808976384 | bytes 6694913 | tf_op jit(solution)/shard_map/while/body/eval_jaxpr/dot_general | solution.py:26
  105.8 0.0 copy-start.1
  105.9 0.0 reduce-scatter.2.cloned.1.call-update
  105.9 8.5 %reduce-scatter.2.cloned.1.call-done = f32[2048,128]{1,0:T(8,128)} async-done(((f32[2048,256]{1,0:T(8,128)}), f32[2048,128]{1,0:T(8,128)}) %reduce-scatter.2.cloned.1.call-update) | async-done | bytes 1048592 | tf_op jit(solution)/shard_map/reduce_scatter | solution.py:46
  114.4 0.0 copy-done.1
  114.4 2.3 %sub.11 = f32[2048,128]{1,0:T(8,128)} subtract(f32[2048,128]{1,0:T(8,128)S(1)} %copy-done.1, f32[2048,128]{1,0:T(8,128)} %reduce-scatter.2.cloned.1.call-done) | non-fusion elementwise | flops 262144 | bytes 3145728 | tf_op jit(solution)/shard_map/sub | solution.py:47
  (18 shorter events, 0.2 us)
Async XLA Ops:
  6.5 51.0 %copy-start.2 = (bf16[128,256]{1,0:T(8,128)(2,1)S(1)}, bf16[128,256]{1,0:T(8,128)(2,1)}, u32[]{:S(2)}) copy-start(bf16[128,256]{1,0:T(8,128)(2,1)} %param.8) | copy-start | bytes 196612
  6.5 78.7 %all-gather.2.cloned.1.call-start = ((), (), s32[]{:S(2)}) async-start(), calls=%async_computation.1 | async-start | bytes 1179648 | tf_op jit(solution)/shard_map/all_gather | solution.py:34
  6.5 8.5 %collective-permute-start = (bf16[128,256]{1,0:T(8,128)(2,1)}, bf16[128,256]{1,0:T(8,128)(2,1)S(1)}, u32[]{:S(2)}, u32[]{:S(2)}) collective-permute-start(bf16[128,256]{1,0:T(8,128)(2,1)} %param.8), channel_id=1, source_target_pairs={{0,2},{2,4},{4,6},{6,8},{8,10},{10,12},{12,14},{14,0},{1,3},{3,5},... | collective-permute-start | bytes 196616 | tf_op jit(solution)/shard_map/ppermute | solution.py:12
  15.1 7.0 %collective-permute-start.1 = (bf16[128,256]{1,0:T(8,128)(2,1)S(1)}, bf16[128,256]{1,0:T(8,128)(2,1)S(1)}, u32[]{:S(2)}, u32[]{:S(2)}) collective-permute-start(bf16[128,256]{1,0:T(8,128)(2,1)S(1)} %collective-permute-done), channel_id=1, source_target_pairs={{0,2},{2,4},{4,6},{6,8},{8,10},{10,12},{12,14},{14,0},{1,3},{3,5},... | collective-permute-start | bytes 196616 | tf_op jit(solution)/shard_map/ppermute | solution.py:12
  22.0 7.0 %collective-permute-start.2 = (bf16[128,256]{1,0:T(8,128)(2,1)S(1)}, bf16[128,256]{1,0:T(8,128)(2,1)S(1)}, u32[]{:S(2)}, u32[]{:S(2)}) collective-permute-start(bf16[128,256]{1,0:T(8,128)(2,1)S(1)} %collective-permute-done.1), channel_id=1, source_target_pairs={{0,2},{2,4},{4,6},{6,8},{8,10},{10,12},{12,14},{14,0},{1,3},{3,5},... | collective-permute-start | bytes 196616 | tf_op jit(solution)/shard_map/ppermute | solution.py:12
  29.0 7.0 %collective-permute-start.3 = (bf16[128,256]{1,0:T(8,128)(2,1)S(1)}, bf16[128,256]{1,0:T(8,128)(2,1)S(1)}, u32[]{:S(2)}, u32[]{:S(2)}) collective-permute-start(bf16[128,256]{1,0:T(8,128)(2,1)S(1)} %collective-permute-done.2), channel_id=1, source_target_pairs={{0,2},{2,4},{4,6},{6,8},{8,10},{10,12},{12,14},{14,0},{1,3},{3,5},... | collective-permute-start | bytes 196616 | tf_op jit(solution)/shard_map/ppermute | solution.py:12
  36.0 7.4 %collective-permute-start.4 = (bf16[128,256]{1,0:T(8,128)(2,1)S(1)}, bf16[128,256]{1,0:T(8,128)(2,1)S(1)}, u32[]{:S(2)}, u32[]{:S(2)}) collective-permute-start(bf16[128,256]{1,0:T(8,128)(2,1)S(1)} %collective-permute-done.3), channel_id=1, source_target_pairs={{0,2},{2,4},{4,6},{6,8},{8,10},{10,12},{12,14},{14,0},{1,3},{3,5},... | collective-permute-start | bytes 196616 | tf_op jit(solution)/shard_map/ppermute | solution.py:12
  43.4 7.0 %collective-permute-start.5 = (bf16[128,256]{1,0:T(8,128)(2,1)S(1)}, bf16[128,256]{1,0:T(8,128)(2,1)S(1)}, u32[]{:S(2)}, u32[]{:S(2)}) collective-permute-start(bf16[128,256]{1,0:T(8,128)(2,1)S(1)} %collective-permute-done.4), channel_id=1, source_target_pairs={{0,2},{2,4},{4,6},{6,8},{8,10},{10,12},{12,14},{14,0},{1,3},{3,5},... | collective-permute-start | bytes 196616 | tf_op jit(solution)/shard_map/ppermute | solution.py:12
  43.4 71.0 %reduce-scatter.2.cloned.1.call-start = ((), (), s32[]{:S(2)}) async-start(), calls=%async_computation.2 | async-start | bytes 3145728 | tf_op jit(solution)/shard_map/reduce_scatter | solution.py:46
  50.3 7.1 %collective-permute-start.6 = (bf16[128,256]{1,0:T(8,128)(2,1)S(1)}, bf16[128,256]{1,0:T(8,128)(2,1)S(1)}, u32[]{:S(2)}, u32[]{:S(2)}) collective-permute-start(bf16[128,256]{1,0:T(8,128)(2,1)S(1)} %collective-permute-done.5), channel_id=1, source_target_pairs={{0,2},{2,4},{4,6},{6,8},{8,10},{10,12},{12,14},{14,0},{1,3},{3,5},... | collective-permute-start | bytes 196616 | tf_op jit(solution)/shard_map/ppermute | solution.py:12
  52.4 32.9 %copy-start = (bf16[2048,512]{1,0:T(8,128)(2,1)S(1)}, bf16[2048,512]{1,0:T(8,128)(2,1)}, u32[]{:S(2)}) copy-start(bf16[2048,512]{1,0:T(8,128)(2,1)} %param.6) | copy-start | bytes 6291460
  105.8 8.5 %copy-start.1 = (f32[2048,128]{1,0:T(8,128)S(1)}, f32[2048,128]{1,0:T(8,128)}, u32[]{:S(2)}) copy-start(f32[2048,128]{1,0:T(8,128)} %param.9) | copy-start | bytes 3145732
Sparse Core Ops, SparseCore 0:
  43.5 41.7 all-gather.1
  106.0 8.3 reduce-scatter.1
